TPU v7x, 256 devices: a whole 4x4x8 slice. The times are simulated.
256 devices in a mesh: seq: 16 (over z, core), head: 16 (over y, x).
Axes of the slice: x: 4, y: 4, z: 8, core: 2. Of those that a mesh axis runs over, the one named last changes fastest.
Arguments:
- queries: bfloat16 [49152, 4096], P(('seq', 'head')), may hold values from -6 to 6
- keys: bfloat16 [49152, 4096], P(('seq', 'head')), may hold values from -6 to 6
- values: bfloat16 [49152, 4096], P(('seq', 'head')), may hold values from -6 to 6
- grad_out: bfloat16 [49152, 4096], P(('seq', 'head')), may hold values from -6 to 6
Outputs:
- attended: bfloat16 [49152, 4096], P(('seq', 'head'))
- grad_queries: bfloat16 [49152, 4096], P(('seq', 'head'))
- grad_keys: bfloat16 [49152, 4096], P(('seq', 'head'))
- grad_values: bfloat16 [49152, 4096], P(('seq', 'head'))
All inputs are finite; a program needn't handle non-finite values.
Results may differ from a plain program's by a relative error of at most 0.005.
Values may be sent and summed in bfloat16 or wider, within the bound.
A program may use at most 128 MiB of HBM per device.

v0:
```python
import math

import jax
import jax.numpy as jnp
from jax import lax
from jax.sharding import PartitionSpec as P

HD = 128
BLOCK = 256


def carried_in(x, axis, combine, identity, reverse):
    peers, mine = (lax.axis_size(axis), lax.axis_index(axis))
    everything = lax.all_gather(x, axis)
    start = jnp.broadcast_to(jnp.asarray(identity, x.dtype), x.shape)

    def turn(k, before):
        at = peers - 1 - k if reverse else k
        reached = at > mine if reverse else at < mine
        new = combine(before, everything[at])
        return jnp.where(reached, new, before)

    return lax.fori_loop(0, peers, turn, start)


def add_states(earlier, later):
    return earlier + later


def on_device(queries, keys, values, grad_out):
    f32 = jnp.float32
    bf16 = jnp.bfloat16
    q_in, k_in, v_in, g_in = (
        lax.all_to_all(queries, "head", split_axis=1, concat_axis=0, tiled=True),
        lax.all_to_all(keys, "head", split_axis=1, concat_axis=0, tiled=True),
        lax.all_to_all(values, "head", split_axis=1, concat_axis=0, tiled=True),
        lax.all_to_all(grad_out, "head", split_axis=1, concat_axis=0, tiled=True),
    )
    rows = q_in.shape[0]
    heads_local = q_in.shape[1] // HD
    blocks = rows // BLOCK
    shape4 = (blocks, BLOCK, heads_local, HD)
    qs = q_in.reshape(shape4)
    ks = k_in.reshape(shape4)
    vs = v_in.reshape(shape4)
    gs = g_in.reshape(shape4)
    scale = 1.0 / math.sqrt(HD * rows * lax.axis_size("seq"))
    kv_blocks = jnp.einsum("bshd,bshe->bhde", ks, vs, preferred_element_type=f32)
    rq_blocks = jnp.einsum("bthi,bthj->bhij", gs, qs, preferred_element_type=f32)
    kv_total = jnp.sum(kv_blocks, axis=0)
    rq_total = jnp.sum(rq_blocks, axis=0)
    zeros = jnp.zeros_like(kv_total)
    kv_before = carried_in(kv_total, "seq", add_states, zeros, False)
    rq_after = carried_in(rq_total, "seq", add_states, zeros, True)
    kv_state = kv_before + (jnp.cumsum(kv_blocks, axis=0) - kv_blocks)
    rq_state = rq_after + (rq_total - jnp.cumsum(rq_blocks, axis=0))
    kv_round = kv_state.astype(bf16)
    rq_round = rq_state.astype(bf16)
    later = lax.broadcasted_iota(jnp.int32, (BLOCK, BLOCK), 0)
    earlier = lax.broadcasted_iota(jnp.int32, (BLOCK, BLOCK), 1)
    mask = (later >= earlier).astype(f32)
    qk = (jnp.einsum("bthd,bshd->bhts", qs, ks, preferred_element_type=f32) * mask).astype(bf16)
    gv = (jnp.einsum("bthd,bshd->bhts", gs, vs, preferred_element_type=f32) * mask).astype(bf16)
    flat = (rows, heads_local * HD)
    attended = scale * (
        jnp.einsum("bhts,bshd->bthd", qk, vs, preferred_element_type=f32)
        + jnp.einsum("bthd,bhde->bthe", qs, kv_round, preferred_element_type=f32)
    )
    attended = attended.astype(bf16).reshape(flat)
    grad_q = scale * (
        jnp.einsum("bhts,bshd->bthd", gv, ks, preferred_element_type=f32)
        + jnp.einsum("bthi,bhji->bthj", gs, kv_round, preferred_element_type=f32)
    )
    grad_q = grad_q.astype(bf16).reshape(flat)
    grad_k = scale * (
        jnp.einsum("bhts,bthd->bshd", gv, qs, preferred_element_type=f32)
        + jnp.einsum("bshi,bhij->bshj", vs, rq_round, preferred_element_type=f32)
    )
    grad_k = grad_k.astype(bf16).reshape(flat)
    grad_v = scale * (
        jnp.einsum("bhts,bthi->bshi", qk, gs, preferred_element_type=f32)
        + jnp.einsum("bshj,bhij->bshi", ks, rq_round, preferred_element_type=f32)
    )
    grad_v = grad_v.astype(bf16).reshape(flat)
    out_a, out_q, out_k, out_v = (
        lax.all_to_all(attended, "head", split_axis=0, concat_axis=1, tiled=True),
        lax.all_to_all(grad_q, "head", split_axis=0, concat_axis=1, tiled=True),
        lax.all_to_all(grad_k, "head", split_axis=0, concat_axis=1, tiled=True),
        lax.all_to_all(grad_v, "head", split_axis=0, concat_axis=1, tiled=True),
    )
    return (out_a, out_q, out_k, out_v)


def solution(mesh):
    in_specs = (
        P(("seq", "head"), None),
        P(("seq", "head"), None),
        P(("seq", "head"), None),
        P(("seq", "head"), None),
    )
    out_specs = (
        P(("seq", "head"), None),
        P(("seq", "head"), None),
        P(("seq", "head"), None),
        P(("seq", "head"), None),
    )
    return jax.shard_map(
        on_device, mesh=mesh, in_specs=in_specs, out_specs=out_specs, check_vma=False
    )
```

profile of v0, /device:TPU:1, one launch (start us, length us, event | category | flops | bytes accessed | tf_op | source)
XLA Modules:
  0.0 297.5 jit_solution(16149724626339038639)
XLA Ops:
  9.9 7.7 %all-to-all-start.1 = ((bf16[192,16,256]{2,0,1:T(8,128)(2,1)}), bf16[192,16,256]{2,0,1:T(8,128)(2,1)S(1)}, u32[]{:S(2)}, u32[]{:S(2)}) async-start(bf16[192,16,256]{2,0,1:T(8,128)(2,1)} %bitcast.78), calls=%async_computation.1 | async-start | bytes 3145728 | tf_op jit(solution)/shard_map/all_to_all | solution.py:35
  18.9 21.6 %all-to-all-done.1 = bf16[192,16,256]{2,0,1:T(8,128)(2,1)S(1)} async-done(((bf16[192,16,256]{2,0,1:T(8,128)(2,1)}), bf16[192,16,256]{2,0,1:T(8,128)(2,1)S(1)}, u32[]{:S(2)}, u32[]{:S(2)}) %all-to-all-start.1) | async-done | bytes 1572896 | tf_op jit(solution)/shard_map/all_to_all | solution.py:35
  40.5 4.6 %all-to-all-start.2 = ((bf16[192,16,256]{2,0,1:T(8,128)(2,1)}), bf16[192,16,256]{2,0,1:T(8,128)(2,1)S(1)}, u32[]{:S(2)}, u32[]{:S(2)}) async-start(bf16[192,16,256]{2,0,1:T(8,128)(2,1)} %bitcast.87), calls=%async_computation.2 | async-start | bytes 3145728 | tf_op jit(solution)/shard_map/all_to_all | solution.py:36
  47.8 18.2 %all-to-all-done.2 = bf16[192,16,256]{2,0,1:T(8,128)(2,1)S(1)} async-done(((bf16[192,16,256]{2,0,1:T(8,128)(2,1)}), bf16[192,16,256]{2,0,1:T(8,128)(2,1)S(1)}, u32[]{:S(2)}, u32[]{:S(2)}) %all-to-all-start.2) | async-done | bytes 1572896 | tf_op jit(solution)/shard_map/all_to_all | solution.py:36
  67.1 6.3 %all-to-all-start = ((bf16[192,16,256]{2,0,1:T(8,128)(2,1)}), bf16[192,16,256]{2,0,1:T(8,128)(2,1)}, u32[]{:S(2)}, u32[]{:S(2)}) async-start(bf16[192,16,256]{2,0,1:T(8,128)(2,1)} %bitcast.79), calls=%async_computation | async-start | bytes 3145728 | tf_op jit(solution)/shard_map/all_to_all | solution.py:34
  81.6 12.6 %all-to-all-done = bf16[192,16,256]{2,0,1:T(8,128)(2,1)} async-done(((bf16[192,16,256]{2,0,1:T(8,128)(2,1)}), bf16[192,16,256]{2,0,1:T(8,128)(2,1)}, u32[]{:S(2)}, u32[]{:S(2)}) %all-to-all-start) | async-done | bytes 1572896 | tf_op jit(solution)/shard_map/all_to_all | solution.py:34
  94.2 6.0 %all-to-all-start.4 = ((bf16[192,16,256]{2,0,1:T(8,128)(2,1)}), bf16[192,16,256]{2,0,1:T(8,128)(2,1)}, u32[]{:S(2)}, u32[]{:S(2)}) async-start(bf16[192,16,256]{2,0,1:T(8,128)(2,1)} %bitcast.76), calls=%async_computation.4 | async-start | bytes 3145728 | tf_op jit(solution)/shard_map/all_to_all | solution.py:37
  103.3 17.1 %all-to-all-done.4 = bf16[192,16,256]{2,0,1:T(8,128)(2,1)} async-done(((bf16[192,16,256]{2,0,1:T(8,128)(2,1)}), bf16[192,16,256]{2,0,1:T(8,128)(2,1)}, u32[]{:S(2)}, u32[]{:S(2)}) %all-to-all-start.4) | async-done | bytes 1572896 | tf_op jit(solution)/shard_map/all_to_all | solution.py:37
  120.4 3.5 %reshape.70 = bf16[12,256,2,128]{3,2,1,0:T(2,128)(2,1)} reshape(bf16[16,192,256]{2,1,0:T(8,128)(2,1)} %bitcast.7) | data formatting | bytes 3145728 | tf_op jit(solution)/shard_map/reshape | solution.py:46
  123.9 4.0 %fusion.32 = (f32[2,128,128]{2,1,0:T(8,128)}, f32[12,2,128,128]{3,2,1,0:T(8,128)}) fusion(bf16[12,256,2,128]{3,2,1,0:T(2,128)(2,1)S(1)} %reshape.67, bf16[12,256,2,128]{3,2,1,0:T(2,128)(2,1)} %reshape.70), kind=kOutput, calls=%fused_computation.47 | convolution fusion | flops 201687040 | bytes 4849664 | tf_op jit(solution)/shard_map/bthi,bthj->bhij/dot_general | solution.py:49
  134.7 15.6 %while.30 = (s32[]{:T(128)}, f32[2,128,128]{2,1,0:T(8,128)S(1)}, s32[]{:T(128)}, f32[16,2,128,128]{3,2,1,0:T(8,128)}, s32[]{:T(128)}, /*index=5*/s32[]{:T(128)}) while((s32[]{:T(128)}, f32[2,128,128]{2,1,0:T(8,128)S(1)}, s32[]{:T(128)}, f32[16,2,128,128]{3,2,1,0:T(8,128)}, s32[]{:T(128)}, /*index=5*/s32[]{:T(128)}) %tuple.84), condition=%wide.region_2.3_spmd.clone, body=%wide.region_1.0_spmd.clone.sunk | while | flops 98308 | bytes 393317 | solution.py:23
  157.0 3.8 %all_to_all.113 = bf16[16,192,256]{2,1,0:T(8,128)(2,1)} reshape(bf16[12,256,2,128]{3,2,1,0:T(2,128)(2,1)} %copy.97) | data formatting | bytes 3145728 | tf_op jit(solution)/shard_map/all_to_all | solution.py:86
  160.8 5.4 %all-to-all-start.3 = ((bf16[16,192,256]{2,1,0:T(8,128)(2,1)}), bf16[16,192,256]{2,1,0:T(8,128)(2,1)}, u32[]{:S(2)}, u32[]{:S(2)}) async-start(bf16[16,192,256]{2,1,0:T(8,128)(2,1)} %all_to_all.113), calls=%async_computation.3 | async-start | bytes 3145728 | tf_op jit(solution)/shard_map/all_to_all | solution.py:86
  166.2 11.4 %all-gather.7.cloned.1.call-done = f32[32,128,128]{2,1,0:T(8,128)} async-done(((f32[2,128,128]{2,1,0:T(8,128)}), f32[32,128,128]{2,1,0:T(8,128)}) %all-gather.7.cloned.1.call-update) | async-done | bytes 2097168 | tf_op jit(solution)/shard_map/all_gather | solution.py:14
  177.5 15.7 %while.31 = (s32[]{:T(128)}, f32[2,128,128]{2,1,0:T(8,128)S(1)}, s32[]{:T(128)}, f32[16,2,128,128]{3,2,1,0:T(8,128)}, s32[]{:T(128)}, /*index=5*/s32[]{:T(128)}, s32[]{:T(128)}, s32[]{:T(128)}) while((s32[]{:T(128)}, f32[2,128,128]{2,1,0:T(8,128)S(1)}, s32[]{:T(128)}, f32[16,2,128,128]{3,2,1,0:T(8,128)}, s32[]{:T(128)}, ...), condition=%wide.region_6.7_spmd.clone, body=%wide.region_5.6_spmd.clone.sunk | while | flops 98312 | bytes 393379 | solution.py:23
  201.0 3.8 %all_to_all.128 = bf16[16,192,256]{2,1,0:T(8,128)(2,1)} reshape(bf16[12,256,2,128]{3,2,1,0:T(2,128)(2,1)} %copy.120) | data formatting | bytes 3145728 | tf_op jit(solution)/shard_map/all_to_all | solution.py:89
  204.8 6.7 %all-to-all-start.7 = ((bf16[16,192,256]{2,1,0:T(8,128)(2,1)}), bf16[16,192,256]{2,1,0:T(8,128)(2,1)}, u32[]{:S(2)}, u32[]{:S(2)}) async-start(bf16[16,192,256]{2,1,0:T(8,128)(2,1)} %all_to_all.128), calls=%async_computation.7 | async-start | bytes 3145728 | tf_op jit(solution)/shard_map/all_to_all | solution.py:89
  220.5 3.7 %all_to_all.124 = bf16[16,192,256]{2,1,0:T(8,128)(2,1)} reshape(bf16[12,256,2,128]{3,2,1,0:T(2,128)(2,1)} %copy.114) | data formatting | bytes 3145728 | tf_op jit(solution)/shard_map/all_to_all | solution.py:88
  224.3 11.9 %all-to-all-done.7 = bf16[16,192,256]{2,1,0:T(8,128)(2,1)} async-done(((bf16[16,192,256]{2,1,0:T(8,128)(2,1)}), bf16[16,192,256]{2,1,0:T(8,128)(2,1)}, u32[]{:S(2)}, u32[]{:S(2)}) %all-to-all-start.7) | async-done | bytes 1572896 | tf_op jit(solution)/shard_map/all_to_all | solution.py:89
  236.2 4.4 %all-to-all-start.6 = ((bf16[16,192,256]{2,1,0:T(8,128)(2,1)}), bf16[16,192,256]{2,1,0:T(8,128)(2,1)}, u32[]{:S(2)}, u32[]{:S(2)}) async-start(bf16[16,192,256]{2,1,0:T(8,128)(2,1)} %all_to_all.124), calls=%async_computation.6 | async-start | bytes 3145728 | tf_op jit(solution)/shard_map/all_to_all | solution.py:88
  240.6 3.0 %fusion.22 = f32[12,2,256,128]{3,2,1,0:T(8,128)S(1)} fusion(bf16[12,2,256,256]{3,2,1,0:T(8,128)(2,1)} %copy-done.5, bf16[12,256,2,128]{3,2,1,0:T(2,128)(2,1)S(1)} %reshape.68), kind=kOutput, calls=%fused_computation.36 | convolution fusion | flops 402653184 | bytes 7864320 | tf_op jit(solution)/shard_map/bhts,bshd->bthd/dot_general | solution.py:71
  248.2 13.8 %all-to-all-done.6 = bf16[16,192,256]{2,1,0:T(8,128)(2,1)} async-done(((bf16[16,192,256]{2,1,0:T(8,128)(2,1)}), bf16[16,192,256]{2,1,0:T(8,128)(2,1)}, u32[]{:S(2)}, u32[]{:S(2)}) %all-to-all-start.6) | async-done | bytes 1572896 | tf_op jit(solution)/shard_map/all_to_all | solution.py:88
  262.0 6.0 %all-to-all-start.5 = ((bf16[16,192,256]{2,1,0:T(8,128)(2,1)}), bf16[16,192,256]{2,1,0:T(8,128)(2,1)S(1)}, u32[]{:S(2)}, u32[]{:S(2)}) async-start(bf16[16,192,256]{2,1,0:T(8,128)(2,1)} %all_to_all.120), calls=%async_computation.5 | async-start | bytes 3145728 | tf_op jit(solution)/shard_map/all_to_all | solution.py:87
  276.2 13.2 %all-to-all-done.5 = bf16[16,192,256]{2,1,0:T(8,128)(2,1)S(1)} async-done(((bf16[16,192,256]{2,1,0:T(8,128)(2,1)}), bf16[16,192,256]{2,1,0:T(8,128)(2,1)S(1)}, u32[]{:S(2)}, u32[]{:S(2)}) %all-to-all-start.5) | async-done | bytes 1572896 | tf_op jit(solution)/shard_map/all_to_all | solution.py:87
  (101 shorter events, 93.8 us)
Async XLA Ops:
  9.9 7.7 %copy-start.14 = (bf16[192,4096]{1,0:T(8,128)(2,1)S(1)}, bf16[192,4096]{1,0:T(8,128)(2,1)}, u32[]{:S(2)}) copy-start(bf16[192,4096]{1,0:T(8,128)(2,1)} %param.10) | copy-start | bytes 4718596
  9.9 30.6 %all-to-all-start.1 = ((bf16[192,16,256]{2,0,1:T(8,128)(2,1)}), bf16[192,16,256]{2,0,1:T(8,128)(2,1)S(1)}, u32[]{:S(2)}, u32[]{:S(2)}) async-start(bf16[192,16,256]{2,0,1:T(8,128)(2,1)} %bitcast.78), calls=%async_computation.1 | async-start | bytes 3145728 | tf_op jit(solution)/shard_map/all_to_all | solution.py:35
  40.5 25.5 %all-to-all-start.2 = ((bf16[192,16,256]{2,0,1:T(8,128)(2,1)}), bf16[192,16,256]{2,0,1:T(8,128)(2,1)S(1)}, u32[]{:S(2)}, u32[]{:S(2)}) async-start(bf16[192,16,256]{2,0,1:T(8,128)(2,1)} %bitcast.87), calls=%async_computation.2 | async-start | bytes 3145728 | tf_op jit(solution)/shard_map/all_to_all | solution.py:36
  66.0 1.1 copy-start.11
  67.1 27.1 %all-to-all-start = ((bf16[192,16,256]{2,0,1:T(8,128)(2,1)}), bf16[192,16,256]{2,0,1:T(8,128)(2,1)}, u32[]{:S(2)}, u32[]{:S(2)}) async-start(bf16[192,16,256]{2,0,1:T(8,128)(2,1)} %bitcast.79), calls=%async_computation | async-start | bytes 3145728 | tf_op jit(solution)/shard_map/all_to_all | solution.py:34
  73.4 61.3 %all-gather.5.cloned.1.call-start = ((), (), s32[]{:S(2)}) async-start(), calls=%async_computation.8 | async-start | bytes 2228224 | tf_op jit(solution)/shard_map/all_gather | solution.py:14
  76.3 2.5 copy-start
  94.2 26.3 %all-to-all-start.4 = ((bf16[192,16,256]{2,0,1:T(8,128)(2,1)}), bf16[192,16,256]{2,0,1:T(8,128)(2,1)}, u32[]{:S(2)}, u32[]{:S(2)}) async-start(bf16[192,16,256]{2,0,1:T(8,128)(2,1)} %bitcast.76), calls=%async_computation.4 | async-start | bytes 3145728 | tf_op jit(solution)/shard_map/all_to_all | solution.py:37
  100.1 77.4 %all-gather.7.cloned.1.call-start = ((), (), s32[]{:S(2)}) async-start(), calls=%async_computation.9 | async-start | bytes 2228224 | tf_op jit(solution)/shard_map/all_gather | solution.py:14
  123.9 4.0 %copy-start.12 = (f32[256,256]{1,0:T(8,128)S(1)}, f32[256,256]{1,0:T(8,128)}, u32[]{:S(2)}) copy-start(f32[256,256]{1,0:T(8,128)} %fusion.30) | copy-start | bytes 786436
  127.9 1.4 copy-start.3
  129.3 2.7 copy-start.1
  150.3 3.3 %copy-start.6 = (f32[12,2,256,128]{3,2,1,0:T(8,128)S(1)}, f32[12,2,256,128]{3,2,1,0:T(8,128)}, u32[]{:S(2)}) copy-start(f32[12,2,256,128]{3,2,1,0:T(8,128)} %fusion.18) | copy-start | bytes 9437188
  160.8 44.0 %all-to-all-start.3 = ((bf16[16,192,256]{2,1,0:T(8,128)(2,1)}), bf16[16,192,256]{2,1,0:T(8,128)(2,1)}, u32[]{:S(2)}, u32[]{:S(2)}) async-start(bf16[16,192,256]{2,1,0:T(8,128)(2,1)} %all_to_all.113), calls=%async_computation.3 | async-start | bytes 3145728 | tf_op jit(solution)/shard_map/all_to_all | solution.py:86
  166.1 27.1 %copy-start.15 = (f32[2,128,128]{2,1,0:T(8,128)S(1)}, f32[2,128,128]{2,1,0:T(8,128)}, u32[]{:S(2)}) copy-start(f32[2,128,128]{2,1,0:T(8,128)} %get-tuple-element.243) | copy-start | bytes 393220
  204.8 6.7 %copy-start.13 = (f32[256,256]{1,0:T(8,128)S(1)}, f32[256,256]{1,0:T(8,128)}, u32[]{:S(2)}) copy-start(f32[256,256]{1,0:T(8,128)} %fusion.30) | copy-start | bytes 786436
  204.8 31.4 %all-to-all-start.7 = ((bf16[16,192,256]{2,1,0:T(8,128)(2,1)}), bf16[16,192,256]{2,1,0:T(8,128)(2,1)}, u32[]{:S(2)}, u32[]{:S(2)}) async-start(bf16[16,192,256]{2,1,0:T(8,128)(2,1)} %all_to_all.128), calls=%async_computation.7 | async-start | bytes 3145728 | tf_op jit(solution)/shard_map/all_to_all | solution.py:89
  214.4 1.6 copy-start.5
  214.4 2.5 copy-start.2
  214.4 2.7 copy-start.8
  236.2 25.8 %all-to-all-start.6 = ((bf16[16,192,256]{2,1,0:T(8,128)(2,1)}), bf16[16,192,256]{2,1,0:T(8,128)(2,1)}, u32[]{:S(2)}, u32[]{:S(2)}) async-start(bf16[16,192,256]{2,1,0:T(8,128)(2,1)} %all_to_all.124), calls=%async_computation.6 | async-start | bytes 3145728 | tf_op jit(solution)/shard_map/all_to_all | solution.py:88
  240.6 3.0 %copy-start.4 = (bf16[12,256,2,128]{3,2,1,0:T(2,128)(2,1)S(1)}, bf16[12,256,2,128]{3,2,1,0:T(2,128)(2,1)}, u32[]{:S(2)}) copy-start(bf16[12,256,2,128]{3,2,1,0:T(2,128)(2,1)} %reshape.70) | copy-start | bytes 4718596
  240.6 3.0 %copy-start.10 = (bf16[12,2,128,128]{3,2,1,0:T(8,128)(2,1)S(1)}, bf16[12,2,128,128]{3,2,1,0:T(8,128)(2,1)}, u32[]{:S(2)}) copy-start(bf16[12,2,128,128]{3,2,1,0:T(8,128)(2,1)} %copy-done.9) | copy-start | bytes 2359300
  262.0 27.4 %all-to-all-start.5 = ((bf16[16,192,256]{2,1,0:T(8,128)(2,1)}), bf16[16,192,256]{2,1,0:T(8,128)(2,1)S(1)}, u32[]{:S(2)}, u32[]{:S(2)}) async-start(bf16[16,192,256]{2,1,0:T(8,128)(2,1)} %all_to_all.120), calls=%async_computation.5 | async-start | bytes 3145728 | tf_op jit(solution)/shard_map/all_to_all | solution.py:87
  (2 other events, 1.9 us)
Sparse Core Ops, SparseCore 0:
  79.0 44.2 all-gather.4
  134.8 42.6 all-gather.6
where the time goes:
time: 300 us; the launch traced here: 298 us
  waiting for transfers between devices  120 us (40%)
  local copies, waits for them, and re-layouts  56.1 us (19%)
  starting transfers between devices  47.1 us (16%)
  other arithmetic  35 us (12%)
  matrix products  24.3 us (8%)
  between operations  14.4 us (5%)
    select_n x32, other arithmetic, turn(): return jnp.where(reached, new, before)  30.4 us
    all_to_all x1, waiting for transfers between devices, on_device(): lax.all_to_all(keys, 'head', split_axis=1, concat_axis=0, tiled=True)  21.6 us
    all_to_all x1, waiting for transfers between devices, on_device(): lax.all_to_all(values, 'head', split_axis=1, concat_axis=0, tiled=True)  18.2 us
    all_to_all x1, waiting for transfers between devices, on_device(): lax.all_to_all(grad_out, 'head', split_axis=1, concat_axis=0, tiled=True)  17.1 us
    all_to_all x1, waiting for transfers between devices, on_device(): lax.all_to_all(grad_k, 'head', split_axis=0, concat_axis=1, tiled=True)  13.8 us
    all_to_all x1, waiting for transfers between devices, on_device(): lax.all_to_all(grad_q, 'head', split_axis=0, concat_axis=1, tiled=True)  13.2 us
    all_to_all x1, waiting for transfers between devices, on_device(): lax.all_to_all(queries, 'head', split_axis=1, concat_axis=0, tiled=True)  12.6 us
    all_to_all x1, waiting for transfers between devices, on_device(): lax.all_to_all(grad_v, 'head', split_axis=0, concat_axis=1, tiled=True)  11.9 us
  transfers between devices with their start and end apart: 10, of which 8 were waited for; matrix products, arithmetic and copies ran while one was open for 31% of the time, Pallas kernels for 0%

commit v1 on v0

v1 whole, which is shorter than its diff:
```python
import functools
import math

import jax
import jax.numpy as jnp
from jax import lax
from jax.experimental import pallas as pl
from jax.experimental.pallas import tpu as pltpu
from jax.sharding import PartitionSpec as P

HD = 128
NH = 16
NZ = 8
NC = 2
CH = 4
F32 = jnp.float32
BF16 = jnp.bfloat16
MESH = pl.DeviceIdType.MESH


PLAN = (
    ("L", 0), ("A", 0), ("C", 0), ("L", 1), ("A", 1), ("D", 0), ("C", 1), ("E", 0),
    ("A", 2), ("D", 1), ("C", 2), ("E", 1), ("L", 2), ("A", 3), ("D", 2), ("C", 3), ("E", 2),
    ("D", 3), ("E", 3), ("L", 3), ("G", 0), ("G", 1), ("G", 2), ("G", 3),
)


def contract(a, b, da, db):
    return lax.dot_general(a, b, (((da,), (db,)), ((), ())), preferred_element_type=F32)


def kernel(
    scale,
    q_hbm, k_hbm, v_hbm, g_hbm,
    a_hbm, dq_hbm, dk_hbm, dv_hbm,
    x4, loc, out4,
    mine, xr, xb, xp,
    cs, cr, zs, zr, ds, dr,
    in_sem, out_sem,
    x1s, x1r, c1s, c1r, zss, zrs, c2s, c2r, x2s, x2r,
):
    seq = lax.axis_index("seq")
    head = lax.axis_index("head")
    z = seq // NC
    core = lax.rem(seq, NC)
    chunks = xr.shape[0]
    rows = xr.shape[3]
    tokens = x4.shape[1]
    wide = x4.shape[2] // chunks
    pair = 2 * HD

    ins = (q_hbm, k_hbm, v_hbm, g_hbm)
    outs = (a_hbm, dq_hbm, dk_hbm, dv_hbm)

    def load(c, i):
        cols = pl.ds(c * wide, wide)
        return pltpu.make_async_copy(ins[i].at[:, cols], x4.at[i, :, cols], in_sem.at[c, i])

    def store(c, i):
        cols = pl.ds(c * wide, wide)
        return pltpu.make_async_copy(out4.at[i, :, cols], outs[i].at[:, cols], out_sem.at[c, i])

    def at_z(to):
        return (to * NC + core, head)

    other = (z * NC + 1 - core, head)

    def remote(src, dst, send, recv, to):
        return pltpu.make_async_remote_copy(src, dst, send, recv, device_id=to, device_id_type=MESH)

    def ahead(d):
        return lax.rem(head + d, NH)

    def slot(i):
        return lax.rem(head + NH - i, NH)

    def x_out(c, d):
        to = ahead(d)
        return remote(mine.at[c, to], xr.at[c, d], x1s.at[c], x1r.at[c], (seq, to))

    def xb_out(c, d):
        to = ahead(d)
        return remote(xb.at[c, to], xp.at[c, head], x2s.at[c], x2r.at[c], (seq, to))

    def x_all(c):
        some = pl.ds(1, NH - 1)
        return remote(mine.at[c, some], xr.at[c, some], x1s.at[c], x1r.at[c], (seq, ahead(1)))

    def xb_all(c):
        some = pl.ds(1, NH - 1)
        return remote(xb.at[c, some], xp.at[c, some], x2s.at[c], x2r.at[c], (seq, ahead(1)))

    def c_swap(c):
        return remote(cs.at[c, 1 - core], cr.at[c], c1s.at[c], c1r.at[c], other)

    def z_out(c, to):
        return remote(zs.at[c], zr.at[c, z], zss.at[c, to], zrs.at[c, z], at_z(to))

    def z_in(c, frm):
        return remote(zs.at[c], zr.at[c, frm], zss.at[c, frm], zrs.at[c, frm], at_z(frm))

    def d_swap(c):
        return remote(ds.at[c], dr.at[c], c2s.at[c], c2r.at[c], other)

    def sends_to(to):
        return jnp.logical_or(
            jnp.logical_and(core == 0, to > z), jnp.logical_and(core == 1, to < z)
        )

    def hears_from(frm):
        return jnp.logical_or(
            jnp.logical_and(core == 0, frm < z), jnp.logical_and(core == 1, frm > z)
        )

    barrier = pltpu.get_barrier_semaphore()

    def greet(to):
        pl.semaphore_signal(barrier, inc=1, device_id=to, device_id_type=MESH)

    for d in range(1, NH):
        greet((seq, ahead(d)))
    for d in range(1, NZ):
        greet(at_z(lax.rem(z + d, NZ)))
    greet(other)

    for c in range(chunks):
        for i in range(4):
            load(c, i).start()

    def part(ref, j):
        return ref[:, j * HD : (j + 1) * HD]

    def each_pair(c, act):
        def body(o, carry):
            cols = pl.ds(pl.multiple_of(c * wide + o * pair, pair), pair)
            act(o, cols, [x4[i, :, cols] for i in range(4)])
            return carry

        lax.fori_loop(0, wide // pair, body, 0)

    slots = HD // rows

    def local_states(c):
        def act(o, cols, qkvg):
            q, k, v, g = qkvg
            for j in range(2):
                kv = contract(part(k, j), part(v, j), 0, 0).astype(BF16)
                rq = contract(part(g, j), part(q, j), 0, 0).astype(BF16)
                for r in range(slots):
                    at = (o * 2 + j) * slots + r
                    mine[c, at, 0] = kv[r * rows : (r + 1) * rows]
                    mine[c, at, 1] = rq[r * rows : (r + 1) * rows]

        each_pair(c, act)

    def local_attention(c):
        t = lax.broadcasted_iota(jnp.int32, (tokens, tokens), 0)
        s = lax.broadcasted_iota(jnp.int32, (tokens, tokens), 1)

        def act(o, cols, qkvg):
            zero = jnp.zeros((tokens, tokens), F32)
            for j in range(2):
                qj, kj, vj, gj = (part(r, j) for r in qkvg)
                here = pl.ds(pl.multiple_of(c * wide + o * pair + j * HD, HD), HD)
                qk = jnp.where(t >= s, contract(qj, kj, 1, 1), zero).astype(BF16)
                loc[0, :, here] = contract(qk, vj, 1, 0)
                gv = jnp.where(t >= s, contract(gj, vj, 1, 1), zero).astype(BF16)
                loc[1, :, here] = contract(gv, kj, 1, 0)
                vg = jnp.where(s >= t, contract(vj, gj, 1, 1), zero).astype(BF16)
                loc[2, :, here] = contract(vg, qj, 1, 0)
                kq = jnp.where(s >= t, contract(kj, qj, 1, 1), zero).astype(BF16)
                loc[3, :, here] = contract(kq, gj, 1, 0)

        each_pair(c, act)

    def finish(c):
        def act(o, cols, qkvg):
            q, k, v, g = qkvg
            for j in range(2):
                here = pl.ds(pl.multiple_of(c * wide + o * pair + j * HD, HD), HD)
                at = pl.ds((o * 2 + j) * slots, slots)
                kv = xp[c, at, 0].reshape(HD, HD)
                rq = xp[c, at, 1].reshape(HD, HD)
                terms = (
                    contract(part(q, j), kv, 1, 0),
                    contract(part(g, j), kv, 1, 1),
                    contract(part(v, j), rq, 1, 0),
                    contract(part(k, j), rq, 1, 1),
                )
                for i in range(4):
                    out4[i, :, here] = (scale * (loc[i, :, here] + terms[i])).astype(BF16)

        each_pair(c, act)

    def stage_a(c):
        xr[c, 0] = mine[c, head]
        x_all(c).wait_recv()
        total = xr[c, 0].astype(F32)
        for d in range(1, NH):
            total += xr[c, d].astype(F32)
        cs[c] = total
        c_swap(c).start()

    def stage_c(c):
        c_swap(c).wait_recv()
        zs[c] = cs[c, core] + cr[c]
        for i in range(NZ):
            @pl.when(sends_to(i))
            def _():
                z_out(c, i).start()

    def stage_d(c):
        ds[c] = jnp.zeros_like(ds[c])
        for i in range(NZ):
            @pl.when(hears_from(i))
            def _():
                z_in(c, i).wait_recv()
                ds[c] += zr[c, i]
        zr[c, z] = ds[c]
        ds[c] += cs[c, core]
        d_swap(c).start()

    def stage_e(c):
        d_swap(c).wait_recv()
        for kind in range(2):
            base = jnp.where(core == kind, zr[c, z], dr[c])
            order = range(NH) if kind == 0 else range(NH - 1, -1, -1)
            for i in order:
                xb[c, i, kind] = base.astype(BF16)
                base = base + xr[c, slot(i), kind].astype(F32)
        for d in range(1, NH):
            xb_out(c, d).start()
        xp[c, head] = xb[c, head]

    def stage_g(c):
        xb_all(c).wait_recv()
        finish(c)
        for i in range(4):
            store(c, i).start()

    for c in range(chunks):
        for i in range(4):
            load(c, i).wait()
        local_states(c)
        if c == 0:
            pl.semaphore_wait(barrier, NH + NZ - 1)
        for d in range(1, NH):
            x_out(c, d).start()

    stages = {
        "L": local_attention, "A": stage_a, "C": stage_c, "D": stage_d, "E": stage_e, "G": stage_g,
    }
    for name, c in PLAN:
        stages[name](c)

    for c in range(chunks):
        x_all(c).wait_send()
        c_swap(c).wait_send()
        for i in range(NZ):
            @pl.when(sends_to(i))
            def _():
                z_out(c, i).wait_send()
        d_swap(c).wait_send()
        xb_all(c).wait_send()
        for i in range(4):
            store(c, i).wait()


def on_device(queries, keys, values, grad_out):
    tokens, width = queries.shape
    heads = width // HD
    rows = heads // CH * HD // NH
    devices = lax.axis_size("seq") * lax.axis_size("head")
    scale = 1.0 / math.sqrt(HD * tokens * devices)
    shift = 2.0 ** math.floor(math.log2(scale))
    state = (CH, NH, 2, rows, HD)
    piece = (rows, HD)
    vmem = pltpu.VMEM
    dma = pltpu.SemaphoreType.DMA
    anywhere = pl.BlockSpec(memory_space=pl.ANY)
    macs = tokens * heads * (8 * tokens * HD + 6 * HD * HD)
    results = pl.pallas_call(
        functools.partial(kernel, scale / shift),
        out_shape=[jax.ShapeDtypeStruct((tokens, width), BF16)] * 4,
        in_specs=[anywhere] * 4,
        out_specs=[anywhere] * 4,
        scratch_shapes=[
            vmem((4, tokens, width), BF16),
            vmem((4, tokens, width), F32),
            vmem((4, tokens, width), BF16),
            vmem(state, BF16), vmem(state, BF16), vmem(state, BF16), vmem(state, BF16),
            vmem((CH, 2) + piece, F32), vmem((CH,) + piece, F32),
            vmem((CH,) + piece, F32), vmem((CH, NZ) + piece, F32),
            vmem((CH,) + piece, F32), vmem((CH,) + piece, F32),
            dma((CH, 4)), dma((CH, 4)),
            dma((CH,)), dma((CH,)),
            dma((CH,)), dma((CH,)),
            dma((CH, NZ)), dma((CH, NZ)),
            dma((CH,)), dma((CH,)),
            dma((CH,)), dma((CH,)),
        ],
        compiler_params=pltpu.CompilerParams(
            collective_id=0, has_side_effects=True, vmem_limit_bytes=58 * 2**20
        ),
        cost_estimate=pl.CostEstimate(
            flops=2 * macs, bytes_accessed=16 * tokens * width, transcendentals=0
        ),
    )(queries, keys, values, grad_out)
    return tuple(r * jnp.asarray(shift, BF16) for r in results)


def solution(mesh):
    spec = P(("seq", "head"), None)
    return jax.shard_map(
        on_device, mesh=mesh, in_specs=(spec,) * 4, out_specs=(spec,) * 4, check_vma=False
    )
```

time: 300 us -> 67 us (0.22)
  waiting for transfers between devices: 120 us -> 0 us
  Pallas kernels: 0 us -> 60.3 us
  local copies, waits for them, and re-layouts: 56.1 us -> 0.01 us
  starting transfers between devices: 47.1 us -> 0 us
  other arithmetic: 35 us -> 5.91 us
  matrix products: 24.3 us -> 0 us
  between operations: 14.4 us -> 0.66 us
    all_to_all x8 -> x0, waiting for transfers between devices: 108 us -> none  [the longest x1 21.6 us: on_device(): lax.all_to_all(keys, 'head', split_axis=1, concat_axis=0, tiled=True)]
    pallas_call x0 -> x1, Pallas kernels: none -> 60.3 us  [on_device(): pl.pallas_call(functools.partial(kernel, scale / shift), out_shape=[jax.S...]
    all_to_all x8 -> x0, starting transfers between devices: 47.1 us -> none  [the longest x1 7.72 us: on_device(): lax.all_to_all(keys, 'head', split_axis=1, concat_axis=0, tiled=True)]
    all_to_all x12 -> x0, local copies, waits for them, and re-layouts: 32.5 us -> none  [the longest x2 6.49 us: on_device(): lax.all_to_all(attended, 'head', split_axis=0, concat_axis=1, tiled=True)]
    select_n x32 -> x0, other arithmetic: 30.4 us -> none  [turn(): return jnp.where(reached, new, before)]
    dot_general x12 -> x0, matrix products: 24.3 us -> none  [the longest x1 3.97 us: on_device(): jnp.einsum('bthi,bthj->bhij', gs, qs, preferred_element_type=f32)]
    all_gather x2 -> x0, waiting for transfers between devices: 11.4 us -> none  [carried_in(): everything = lax.all_gather(x, axis)]
    convert_element_type x4 -> x0, local copies, waits for them, and re-layouts: 9.91 us -> none  [the longest x1 2.76 us: on_device(): attended = attended.astype(bf16).reshape(flat)]
  transfers between devices with their start and end apart: 10 -> 0, of which waited for: 8 -> 0; matrix products, arithmetic and copies ran while one was open for 31% -> 0% of each run, Pallas kernels for 0% -> 0%
where the time goes in v1:
time: 67 us; the launch traced here: 66.9 us
  Pallas kernels  60.3 us (90%)
  other arithmetic  5.91 us (9%)
    pallas_call x1, Pallas kernels, on_device(): pl.pallas_call(functools.partial(kernel, scale / shift), out_shape=[jax.S...  60.3 us
    mul x2, other arithmetic, on_device(): return tuple((r * jnp.asarray(shift, BF16) for r in results))  5.91 us

profile of v1, /device:TPU:1, one launch (start us, length us, event | category | flops | bytes accessed | tf_op | source)
XLA Modules:
  0.0 66.9 jit_solution(13844593677943134717)
XLA Ops:
  0.6 60.3 %shard_map.75 = (bf16[192,4096]{1,0:T(8,128)(2,1)}, bf16[192,4096]{1,0:T(8,128)(2,1)}, bf16[192,4096]{1,0:T(8,128)(2,1)}, bf16[192,4096]{1,0:T(8,128)(2,1)}) custom-call(bf16[192,4096]{1,0:T(8,128)(2,1)} %q_hbm.1, bf16[192,4096]{1,0:T(8,128)(2,1)} %k_hbm.1, bf16[192,4096]{1,0:T(8,128)(2,1)} %v_hbm.1, bf16[192,4096]{1,0:T(8,128)(2,1)} %g_hbm.1), custom_call_target="tpu_custom_call" | custom-call | flops 3623878656 | bytes 12582912 | tf_op jit(solution)/shard_map/pallas_call | solution.py:282
  61.0 0.0 copy-start
  61.0 0.0 copy-start.1
  61.0 4.0 %broadcast_multiply_fusion.2 = (bf16[192,4096]{1,0:T(8,128)(2,1)}, bf16[192,4096]{1,0:T(8,128)(2,1)}) fusion(bf16[192,4096]{1,0:T(8,128)(2,1)} %get-tuple-element.9, bf16[192,4096]{1,0:T(8,128)(2,1)} %get-tuple-element.8), kind=kLoop, calls=%fused_computation.2 | loop fusion | flops 1572864 | bytes 6291456 | tf_op jit(solution)/shard_map/mul | solution.py:309
  64.9 0.0 copy-done
  64.9 0.0 copy-done.1
  65.0 1.9 %broadcast_multiply_fusion = (bf16[192,4096]{1,0:T(8,128)(2,1)}, bf16[192,4096]{1,0:T(8,128)(2,1)}) fusion(bf16[192,4096]{1,0:T(8,128)(2,1)S(1)} %copy-done.1, bf16[192,4096]{1,0:T(8,128)(2,1)S(1)} %copy-done), kind=kLoop, calls=%fused_computation | loop fusion | flops 1572864 | bytes 6291456 | tf_op jit(solution)/shard_map/mul | solution.py:309
Async XLA Ops:
  61.0 4.0 %copy-start = (bf16[192,4096]{1,0:T(8,128)(2,1)S(1)}, bf16[192,4096]{1,0:T(8,128)(2,1)}, u32[]{:S(2)}) copy-start(bf16[192,4096]{1,0:T(8,128)(2,1)} %get-tuple-element.10) | copy-start | bytes 4718596
  61.0 4.0 %copy-start.1 = (bf16[192,4096]{1,0:T(8,128)(2,1)S(1)}, bf16[192,4096]{1,0:T(8,128)(2,1)}, u32[]{:S(2)}) copy-start(bf16[192,4096]{1,0:T(8,128)(2,1)} %get-tuple-element.11) | copy-start | bytes 4718596

commit v2 on v1

--- a/solution.py
+++ b/solution.py
@@ -32,11 +32,11 @@
 def kernel(
     scale,
     q_hbm, k_hbm, v_hbm, g_hbm,
-    a_hbm, dq_hbm, dk_hbm, dv_hbm,
-    x4, loc, out4,
+    a_out, dq_out, dk_out, dv_out,
+    x4, loc,
     mine, xr, xb, xp,
     cs, cr, zs, zr, ds, dr,
-    in_sem, out_sem,
+    in_sem,
     x1s, x1r, c1s, c1r, zss, zrs, c2s, c2r, x2s, x2r,
 ):
     seq = lax.axis_index("seq")
@@ -50,15 +50,11 @@
     pair = 2 * HD
 
     ins = (q_hbm, k_hbm, v_hbm, g_hbm)
-    outs = (a_hbm, dq_hbm, dk_hbm, dv_hbm)
+    outs = (a_out, dq_out, dk_out, dv_out)
 
     def load(c, i):
         cols = pl.ds(c * wide, wide)
         return pltpu.make_async_copy(ins[i].at[:, cols], x4.at[i, :, cols], in_sem.at[c, i])
-
-    def store(c, i):
-        cols = pl.ds(c * wide, wide)
-        return pltpu.make_async_copy(out4.at[i, :, cols], outs[i].at[:, cols], out_sem.at[c, i])
 
     def at_z(to):
         return (to * NC + core, head)
@@ -188,7 +184,7 @@
                     contract(part(k, j), rq, 1, 1),
                 )
                 for i in range(4):
-                    out4[i, :, here] = (scale * (loc[i, :, here] + terms[i])).astype(BF16)
+                    outs[i][:, here] = (scale * (loc[i, :, here] + terms[i])).astype(BF16)
 
         each_pair(c, act)
 
@@ -235,8 +231,6 @@
     def stage_g(c):
         xb_all(c).wait_recv()
         finish(c)
-        for i in range(4):
-            store(c, i).start()
 
     for c in range(chunks):
         for i in range(4):
@@ -262,8 +256,6 @@
                 z_out(c, i).wait_send()
         d_swap(c).wait_send()
         xb_all(c).wait_send()
-        for i in range(4):
-            store(c, i).wait()
 
 
 def on_device(queries, keys, values, grad_out):
@@ -281,18 +273,16 @@
     macs = tokens * heads * (8 * tokens * HD + 6 * HD * HD)
     results = pl.pallas_call(
         functools.partial(kernel, scale / shift),
-        out_shape=[jax.ShapeDtypeStruct((tokens, width), BF16)] * 4,
+        out_shape=[pltpu.VMEM((tokens, width), BF16)] * 4,
         in_specs=[anywhere] * 4,
-        out_specs=[anywhere] * 4,
         scratch_shapes=[
             vmem((4, tokens, width), BF16),
             vmem((4, tokens, width), F32),
-            vmem((4, tokens, width), BF16),
             vmem(state, BF16), vmem(state, BF16), vmem(state, BF16), vmem(state, BF16),
             vmem((CH, 2) + piece, F32), vmem((CH,) + piece, F32),
             vmem((CH,) + piece, F32), vmem((CH, NZ) + piece, F32),
             vmem((CH,) + piece, F32), vmem((CH,) + piece, F32),
-            dma((CH, 4)), dma((CH, 4)),
+            dma((CH, 4)),
             dma((CH,)), dma((CH,)),
             dma((CH,)), dma((CH,)),
             dma((CH, NZ)), dma((CH, NZ)),
@@ -300,7 +290,7 @@
             dma((CH,)), dma((CH,)),
         ],
         compiler_params=pltpu.CompilerParams(
-            collective_id=0, has_side_effects=True, vmem_limit_bytes=58 * 2**20
+            collective_id=0, has_side_effects=True, vmem_limit_bytes=54 * 2**20
         ),
         cost_estimate=pl.CostEstimate(
             flops=2 * macs, bytes_accessed=16 * tokens * width, transcendentals=0

time: 67 us -> 63.6 us (0.949)
  other arithmetic: 5.91 us -> 3.88 us
  Pallas kernels: 60.3 us -> 59 us
    mul x2, other arithmetic: 5.91 us -> 3.88 us  [on_device(): return tuple((r * jnp.asarray(shift, BF16) for r in results))]
    pallas_call x1, Pallas kernels: 60.3 us -> 59 us  [on_device(): pl.pallas_call(functools.partial(kernel, scale / shift), out_shape=[pltpu...]
where the time goes in v2:
time: 63.6 us; the launch traced here: 63.5 us
  Pallas kernels  59 us (93%)
  other arithmetic  3.88 us (6%)
  between operations  0.64 us (1%)
    pallas_call x1, Pallas kernels, on_device(): pl.pallas_call(functools.partial(kernel, scale / shift), out_shape=[pltpu...  59 us
    mul x2, other arithmetic, on_device(): return tuple((r * jnp.asarray(shift, BF16) for r in results))  3.88 us

profile of v2, /device:TPU:1, one launch (start us, length us, event | category | flops | bytes accessed | tf_op | source)
XLA Modules:
  0.0 63.5 jit_solution(5799921123853440167)
XLA Ops:
  0.6 59.0 %shard_map.75 = (bf16[192,4096]{1,0:T(8,128)(2,1)S(1)}, bf16[192,4096]{1,0:T(8,128)(2,1)S(1)}, bf16[192,4096]{1,0:T(8,128)(2,1)S(1)}, bf16[192,4096]{1,0:T(8,128)(2,1)S(1)}) custom-call(bf16[192,4096]{1,0:T(8,128)(2,1)} %q_hbm.1, bf16[192,4096]{1,0:T(8,128)(2,1)} %k_hbm.1, bf16[192,4096]{1,0:T(8,128)(2,1)} %v_hbm.1, bf16[192,4096]{1,0:T(8,128)(2,1)} %g_hbm.1), custom_call_target="tpu_custom_call" | custom-call | flops 3623878656 | bytes 12582912 | tf_op jit(solution)/shard_map/pallas_call | solution.py:274
  59.6 1.9 %broadcast_multiply_fusion.2 = (bf16[192,4096]{1,0:T(8,128)(2,1)}, bf16[192,4096]{1,0:T(8,128)(2,1)}) fusion(bf16[192,4096]{1,0:T(8,128)(2,1)S(1)} %get-tuple-element.9, bf16[192,4096]{1,0:T(8,128)(2,1)S(1)} %get-tuple-element.8), kind=kLoop, calls=%fused_computation.2 | loop fusion | flops 1572864 | bytes 6291456 | tf_op jit(solution)/shard_map/mul | solution.py:299
  61.6 1.9 %broadcast_multiply_fusion = (bf16[192,4096]{1,0:T(8,128)(2,1)}, bf16[192,4096]{1,0:T(8,128)(2,1)}) fusion(bf16[192,4096]{1,0:T(8,128)(2,1)S(1)} %get-tuple-element.11, bf16[192,4096]{1,0:T(8,128)(2,1)S(1)} %get-tuple-element.10), kind=kLoop, calls=%fused_computation | loop fusion | flops 1572864 | bytes 6291456 | tf_op jit(solution)/shard_map/mul | solution.py:299

commit v3 on v2

--- a/solution.py
+++ b/solution.py
@@ -9,7 +9,9 @@
 from jax.sharding import PartitionSpec as P
 
 HD = 128
-NH = 16
+NX = 4
+NY = 4
+NH = NX * NY
 NZ = 8
 NC = 2
 CH = 4
@@ -18,10 +20,11 @@
 MESH = pl.DeviceIdType.MESH
 
 
+ORDER = (10, 6, 9, 14, 11, 5, 15, 7, 13, 2, 8, 1, 3, 4, 12)
 PLAN = (
-    ("L", 0), ("A", 0), ("C", 0), ("L", 1), ("A", 1), ("D", 0), ("C", 1), ("E", 0),
-    ("A", 2), ("D", 1), ("C", 2), ("E", 1), ("L", 2), ("A", 3), ("D", 2), ("C", 3), ("E", 2),
-    ("D", 3), ("E", 3), ("L", 3), ("G", 0), ("G", 1), ("G", 2), ("G", 3),
+    ("L", 0), ("A", 0), ("C", 0), ("L", 1), ("A", 1), ("C", 1), ("D", 0), ("E", 0),
+    ("A", 2), ("C", 2), ("D", 1), ("E", 1), ("L", 2), ("A", 3), ("C", 3), ("D", 2),
+    ("E", 2), ("D", 3), ("E", 3), ("L", 3), ("G", 0), ("G", 1), ("G", 2), ("G", 3),
 )
 
 
@@ -36,13 +39,15 @@
     x4, loc,
     mine, xr, xb, xp,
     cs, cr, zs, zr, ds, dr,
-    in_sem,
+    in_sem, told,
     x1s, x1r, c1s, c1r, zss, zrs, c2s, c2r, x2s, x2r,
 ):
     seq = lax.axis_index("seq")
     head = lax.axis_index("head")
     z = seq // NC
     core = lax.rem(seq, NC)
+    y = head // NX
+    x = lax.rem(head, NX)
     chunks = xr.shape[0]
     rows = xr.shape[3]
     tokens = x4.shape[1]
@@ -65,10 +70,10 @@
         return pltpu.make_async_remote_copy(src, dst, send, recv, device_id=to, device_id_type=MESH)
 
     def ahead(d):
-        return lax.rem(head + d, NH)
+        return lax.rem(y + d // NX, NY) * NX + lax.rem(x + d % NX, NX)
 
     def slot(i):
-        return lax.rem(head + NH - i, NH)
+        return lax.rem(y + NY - i // NX, NY) * NX + lax.rem(x + NX - i % NX, NX)
 
     def x_out(c, d):
         to = ahead(d)
@@ -114,9 +119,9 @@
         pl.semaphore_signal(barrier, inc=1, device_id=to, device_id_type=MESH)
 
     for d in range(1, NH):
-        greet((seq, ahead(d)))
+        greet((z * NC, ahead(d)))
     for d in range(1, NZ):
-        greet(at_z(lax.rem(z + d, NZ)))
+        greet((lax.rem(z + d, NZ) * NC + 1, head))
     greet(other)
 
     for c in range(chunks):
@@ -224,7 +229,7 @@
             for i in order:
                 xb[c, i, kind] = base.astype(BF16)
                 base = base + xr[c, slot(i), kind].astype(F32)
-        for d in range(1, NH):
+        for d in ORDER:
             xb_out(c, d).start()
         xp[c, head] = xb[c, head]
 
@@ -237,14 +242,34 @@
             load(c, i).wait()
         local_states(c)
         if c == 0:
-            pl.semaphore_wait(barrier, NH + NZ - 1)
-        for d in range(1, NH):
+            @pl.when(core == 0)
+            def _():
+                pl.semaphore_wait(barrier, NC * (NH - 1) + 1)
+                pl.semaphore_signal(told, inc=1, device_id=other, device_id_type=MESH)
+
+            @pl.when(core == 1)
+            def _():
+                pl.semaphore_wait(told, 1)
+
+        for d in ORDER:
             x_out(c, d).start()
 
     stages = {
         "L": local_attention, "A": stage_a, "C": stage_c, "D": stage_d, "E": stage_e, "G": stage_g,
     }
+    def meet_z():
+        @pl.when(core == 1)
+        def _():
+            pl.semaphore_wait(barrier, NC * (NZ - 1) + 1)
+            pl.semaphore_signal(told, inc=1, device_id=other, device_id_type=MESH)
+
+        @pl.when(core == 0)
+        def _():
+            pl.semaphore_wait(told, 1)
+
     for name, c in PLAN:
+        if (name, c) == ("A", 0):
+            meet_z()
         stages[name](c)
 
     for c in range(chunks):
@@ -282,7 +307,7 @@
             vmem((CH, 2) + piece, F32), vmem((CH,) + piece, F32),
             vmem((CH,) + piece, F32), vmem((CH, NZ) + piece, F32),
             vmem((CH,) + piece, F32), vmem((CH,) + piece, F32),
-            dma((CH, 4)),
+            dma((CH, 4)), pltpu.SemaphoreType.REGULAR,
             dma((CH,)), dma((CH,)),
             dma((CH,)), dma((CH,)),
             dma((CH, NZ)), dma((CH, NZ)),

time: 63.6 us -> 61.2 us (0.962)
  Pallas kernels: 59 us -> 56.6 us
    pallas_call x1, Pallas kernels: 59 us -> 56.6 us  [on_device(): pl.pallas_call(functools.partial(kernel, scale / shift), out_shape=[pltpu...]
where the time goes in v3:
time: 61.2 us
  Pallas kernels  56.6 us (92%)
  other arithmetic  3.88 us (6%)
  between operations  0.64 us (1%)
    pallas_call x1, Pallas kernels, on_device(): pl.pallas_call(functools.partial(kernel, scale / shift), out_shape=[pltpu...  56.6 us
    mul x2, other arithmetic, on_device(): return tuple((r * jnp.asarray(shift, BF16) for r in results))  3.88 us

profile of v3, /device:TPU:1, one launch (start us, length us, event | category | flops | bytes accessed | tf_op | source)
XLA Modules:
  0.0 61.2 jit_solution(12390868481470061218)
XLA Ops:
  0.6 56.6 %shard_map.75 = (bf16[192,4096]{1,0:T(8,128)(2,1)S(1)}, bf16[192,4096]{1,0:T(8,128)(2,1)S(1)}, bf16[192,4096]{1,0:T(8,128)(2,1)S(1)}, bf16[192,4096]{1,0:T(8,128)(2,1)S(1)}) custom-call(bf16[192,4096]{1,0:T(8,128)(2,1)} %q_hbm.1, bf16[192,4096]{1,0:T(8,128)(2,1)} %k_hbm.1, bf16[192,4096]{1,0:T(8,128)(2,1)} %v_hbm.1, bf16[192,4096]{1,0:T(8,128)(2,1)} %g_hbm.1), custom_call_target="tpu_custom_call" | custom-call | flops 3623878656 | bytes 12582912 | tf_op jit(solution)/shard_map/pallas_call | solution.py:299
  57.3 1.9 %broadcast_multiply_fusion.2 = (bf16[192,4096]{1,0:T(8,128)(2,1)}, bf16[192,4096]{1,0:T(8,128)(2,1)}) fusion(bf16[192,4096]{1,0:T(8,128)(2,1)S(1)} %get-tuple-element.9, bf16[192,4096]{1,0:T(8,128)(2,1)S(1)} %get-tuple-element.8), kind=kLoop, calls=%fused_computation.2 | loop fusion | flops 1572864 | bytes 6291456 | tf_op jit(solution)/shard_map/mul | solution.py:324
  59.2 1.9 %broadcast_multiply_fusion = (bf16[192,4096]{1,0:T(8,128)(2,1)}, bf16[192,4096]{1,0:T(8,128)(2,1)}) fusion(bf16[192,4096]{1,0:T(8,128)(2,1)S(1)} %get-tuple-element.11, bf16[192,4096]{1,0:T(8,128)(2,1)S(1)} %get-tuple-element.10), kind=kLoop, calls=%fused_computation | loop fusion | flops 1572864 | bytes 6291456 | tf_op jit(solution)/shard_map/mul | solution.py:324

commit v4 on v3

--- a/solution.py
+++ b/solution.py
@@ -283,13 +283,21 @@
         xb_all(c).wait_send()
 
 
+def write_out(a, dq, dk, dv, a_hbm, dq_hbm, dk_hbm, dv_hbm, sem):
+    pairs = ((a, a_hbm), (dq, dq_hbm), (dk, dk_hbm), (dv, dv_hbm))
+    moves = [pltpu.make_async_copy(src, dst, sem.at[i]) for i, (src, dst) in enumerate(pairs)]
+    for move in moves:
+        move.start()
+    for move in moves:
+        move.wait()
+
+
 def on_device(queries, keys, values, grad_out):
     tokens, width = queries.shape
     heads = width // HD
     rows = heads // CH * HD // NH
     devices = lax.axis_size("seq") * lax.axis_size("head")
     scale = 1.0 / math.sqrt(HD * tokens * devices)
-    shift = 2.0 ** math.floor(math.log2(scale))
     state = (CH, NH, 2, rows, HD)
     piece = (rows, HD)
     vmem = pltpu.VMEM
@@ -297,7 +305,7 @@
     anywhere = pl.BlockSpec(memory_space=pl.ANY)
     macs = tokens * heads * (8 * tokens * HD + 6 * HD * HD)
     results = pl.pallas_call(
-        functools.partial(kernel, scale / shift),
+        functools.partial(kernel, scale),
         out_shape=[pltpu.VMEM((tokens, width), BF16)] * 4,
         in_specs=[anywhere] * 4,
         scratch_shapes=[
@@ -321,7 +329,15 @@
             flops=2 * macs, bytes_accessed=16 * tokens * width, transcendentals=0
         ),
     )(queries, keys, values, grad_out)
-    return tuple(r * jnp.asarray(shift, BF16) for r in results)
+    written = pl.pallas_call(
+        write_out,
+        out_shape=[jax.ShapeDtypeStruct((tokens, width), BF16)] * 4,
+        in_specs=[anywhere] * 4,
+        out_specs=[anywhere] * 4,
+        scratch_shapes=[dma((4,))],
+        compiler_params=pltpu.CompilerParams(vmem_limit_bytes=4 * 2**20),
+    )(*results)
+    return tuple(written)
 
 
 def solution(mesh):

time: 61.2 us -> 60.1 us (0.982)
  other arithmetic: 3.88 us -> 0 us
  Pallas kernels: 56.6 us -> 59.4 us
    mul x2 -> x0, other arithmetic: 3.88 us -> none  [on_device(): return tuple((r * jnp.asarray(shift, BF16) for r in results))]
    pallas_call x1 -> x2, Pallas kernels: 56.6 us -> 59.4 us  [the longest x1 56.6 us: on_device(): pl.pallas_call(functools.partial(kernel, scale), out_shape=[pltpu.VMEM((t...]
where the time goes in v4:
time: 60.1 us; the launch traced here: 60 us
  Pallas kernels  59.4 us (99%)
  between operations  0.64 us (1%)
    pallas_call x1, Pallas kernels, on_device(): pl.pallas_call(functools.partial(kernel, scale), out_shape=[pltpu.VMEM((t...  56.6 us
    pallas_call x1, Pallas kernels, on_device(): pl.pallas_call(write_out, out_shape=[jax.ShapeDtypeStruct((tokens, width)...  2.73 us

profile of v4, /device:TPU:1, one launch (start us, length us, event | category | flops | bytes accessed | tf_op | source)
XLA Modules:
  0.0 60.0 jit_solution(2828440722686504611)
XLA Ops:
  0.6 56.6 %shard_map.75 = (bf16[192,4096]{1,0:T(8,128)(2,1)S(1)}, bf16[192,4096]{1,0:T(8,128)(2,1)S(1)}, bf16[192,4096]{1,0:T(8,128)(2,1)S(1)}, bf16[192,4096]{1,0:T(8,128)(2,1)S(1)}) custom-call(bf16[192,4096]{1,0:T(8,128)(2,1)} %q_hbm.1, bf16[192,4096]{1,0:T(8,128)(2,1)} %k_hbm.1, bf16[192,4096]{1,0:T(8,128)(2,1)} %v_hbm.1, bf16[192,4096]{1,0:T(8,128)(2,1)} %g_hbm.1), custom_call_target="tpu_custom_call" | custom-call | flops 3623878656 | bytes 12582912 | tf_op jit(solution)/shard_map/pallas_call | solution.py:307
  57.3 2.7 %shard_map.76 = (bf16[192,4096]{1,0:T(8,128)(2,1)}, bf16[192,4096]{1,0:T(8,128)(2,1)}, bf16[192,4096]{1,0:T(8,128)(2,1)}, bf16[192,4096]{1,0:T(8,128)(2,1)}) custom-call(bf16[192,4096]{1,0:T(8,128)(2,1)S(1)} %get-tuple-element.8.a, bf16[192,4096]{1,0:T(8,128)(2,1)S(1)} %get-tuple-element.9.dq, bf16[192,4096]{1,0:T(8,128)(2,1)S(1)} %get-tuple-element.10.dk, ...), custom_call_target="tpu_custom_call" | custom-call | tf_op jit(solution)/shard_map/pallas_call | solution.py:332

commit v5 on v4

--- a/solution.py
+++ b/solution.py
@@ -14,7 +14,8 @@
 NH = NX * NY
 NZ = 8
 NC = 2
-CH = 4
+CH = 8
+CHUNKS = ((0, 1), (1, 1), (2, 2), (4, 2), (6, 1), (7, 1))
 F32 = jnp.float32
 BF16 = jnp.bfloat16
 MESH = pl.DeviceIdType.MESH
@@ -23,8 +24,10 @@
 ORDER = (10, 6, 9, 14, 11, 5, 15, 7, 13, 2, 8, 1, 3, 4, 12)
 PLAN = (
     ("L", 0), ("A", 0), ("C", 0), ("L", 1), ("A", 1), ("C", 1), ("D", 0), ("E", 0),
-    ("A", 2), ("C", 2), ("D", 1), ("E", 1), ("L", 2), ("A", 3), ("C", 3), ("D", 2),
-    ("E", 2), ("D", 3), ("E", 3), ("L", 3), ("G", 0), ("G", 1), ("G", 2), ("G", 3),
+    ("L", 2), ("A", 2), ("C", 2), ("D", 1), ("E", 1), ("L", 3), ("A", 3), ("C", 3),
+    ("D", 2), ("E", 2), ("A", 4), ("C", 4), ("D", 3), ("E", 3), ("A", 5), ("C", 5),
+    ("D", 4), ("E", 4), ("D", 5), ("E", 5), ("L", 4), ("L", 5), ("G", 0), ("G", 1),
+    ("G", 2), ("G", 3), ("G", 4), ("G", 5),
 )
 
 
@@ -48,17 +51,20 @@
     core = lax.rem(seq, NC)
     y = head // NX
     x = lax.rem(head, NX)
-    chunks = xr.shape[0]
+    groups = xr.shape[0]
     rows = xr.shape[3]
+    chunks = range(len(CHUNKS))
+    runs = [pl.ds(first, many) for first, many in CHUNKS]
     tokens = x4.shape[1]
-    wide = x4.shape[2] // chunks
+    wide = x4.shape[2] // groups
     pair = 2 * HD
 
     ins = (q_hbm, k_hbm, v_hbm, g_hbm)
     outs = (a_out, dq_out, dk_out, dv_out)
 
     def load(c, i):
-        cols = pl.ds(c * wide, wide)
+        first, many = CHUNKS[c]
+        cols = pl.ds(first * wide, many * wide)
         return pltpu.make_async_copy(ins[i].at[:, cols], x4.at[i, :, cols], in_sem.at[c, i])
 
     def at_z(to):
@@ -77,31 +83,31 @@
 
     def x_out(c, d):
         to = ahead(d)
-        return remote(mine.at[c, to], xr.at[c, d], x1s.at[c], x1r.at[c], (seq, to))
+        return remote(mine.at[runs[c], to], xr.at[runs[c], d], x1s.at[c], x1r.at[c], (seq, to))
 
     def xb_out(c, d):
         to = ahead(d)
-        return remote(xb.at[c, to], xp.at[c, head], x2s.at[c], x2r.at[c], (seq, to))
+        return remote(xb.at[runs[c], to], xp.at[runs[c], head], x2s.at[c], x2r.at[c], (seq, to))
 
     def x_all(c):
         some = pl.ds(1, NH - 1)
-        return remote(mine.at[c, some], xr.at[c, some], x1s.at[c], x1r.at[c], (seq, ahead(1)))
+        return remote(mine.at[runs[c], some], xr.at[runs[c], some], x1s.at[c], x1r.at[c], (seq, ahead(1)))
 
     def xb_all(c):
         some = pl.ds(1, NH - 1)
-        return remote(xb.at[c, some], xp.at[c, some], x2s.at[c], x2r.at[c], (seq, ahead(1)))
+        return remote(xb.at[runs[c], some], xp.at[runs[c], some], x2s.at[c], x2r.at[c], (seq, ahead(1)))
 
     def c_swap(c):
-        return remote(cs.at[c, 1 - core], cr.at[c], c1s.at[c], c1r.at[c], other)
+        return remote(cs.at[runs[c], 1 - core], cr.at[runs[c]], c1s.at[c], c1r.at[c], other)
 
     def z_out(c, to):
-        return remote(zs.at[c], zr.at[c, z], zss.at[c, to], zrs.at[c, z], at_z(to))
+        return remote(zs.at[runs[c]], zr.at[runs[c], z], zss.at[c, to], zrs.at[c, z], at_z(to))
 
     def z_in(c, frm):
-        return remote(zs.at[c], zr.at[c, frm], zss.at[c, frm], zrs.at[c, frm], at_z(frm))
+        return remote(zs.at[runs[c]], zr.at[runs[c], frm], zss.at[c, frm], zrs.at[c, frm], at_z(frm))
 
     def d_swap(c):
-        return remote(ds.at[c], dr.at[c], c2s.at[c], c2r.at[c], other)
+        return remote(ds.at[runs[c]], dr.at[runs[c]], c2s.at[c], c2r.at[c], other)
 
     def sends_to(to):
         return jnp.logical_or(
@@ -124,7 +130,7 @@
         greet((lax.rem(z + d, NZ) * NC + 1, head))
     greet(other)
 
-    for c in range(chunks):
+    for c in chunks:
         for i in range(4):
             load(c, i).start()
 
@@ -132,25 +138,28 @@
         return ref[:, j * HD : (j + 1) * HD]
 
     def each_pair(c, act):
-        def body(o, carry):
-            cols = pl.ds(pl.multiple_of(c * wide + o * pair, pair), pair)
-            act(o, cols, [x4[i, :, cols] for i in range(4)])
+        first, many = CHUNKS[c]
+        each = wide // pair
+
+        def body(i, carry):
+            cols = pl.ds(pl.multiple_of((first * each + i) * pair, pair), pair)
+            act(first + i // each, lax.rem(i, each), [x4[j, :, cols] for j in range(4)])
             return carry
 
-        lax.fori_loop(0, wide // pair, body, 0)
+        lax.fori_loop(0, many * each, body, 0)
 
     slots = HD // rows
 
     def local_states(c):
-        def act(o, cols, qkvg):
+        def act(u, o, qkvg):
             q, k, v, g = qkvg
             for j in range(2):
                 kv = contract(part(k, j), part(v, j), 0, 0).astype(BF16)
                 rq = contract(part(g, j), part(q, j), 0, 0).astype(BF16)
                 for r in range(slots):
                     at = (o * 2 + j) * slots + r
-                    mine[c, at, 0] = kv[r * rows : (r + 1) * rows]
-                    mine[c, at, 1] = rq[r * rows : (r + 1) * rows]
+                    mine[u, at, 0] = kv[r * rows : (r + 1) * rows]
+                    mine[u, at, 1] = rq[r * rows : (r + 1) * rows]
 
         each_pair(c, act)
 
@@ -158,11 +167,11 @@
         t = lax.broadcasted_iota(jnp.int32, (tokens, tokens), 0)
         s = lax.broadcasted_iota(jnp.int32, (tokens, tokens), 1)
 
-        def act(o, cols, qkvg):
+        def act(u, o, qkvg):
             zero = jnp.zeros((tokens, tokens), F32)
             for j in range(2):
                 qj, kj, vj, gj = (part(r, j) for r in qkvg)
-                here = pl.ds(pl.multiple_of(c * wide + o * pair + j * HD, HD), HD)
+                here = pl.ds(pl.multiple_of(u * wide + o * pair + j * HD, HD), HD)
                 qk = jnp.where(t >= s, contract(qj, kj, 1, 1), zero).astype(BF16)
                 loc[0, :, here] = contract(qk, vj, 1, 0)
                 gv = jnp.where(t >= s, contract(gj, vj, 1, 1), zero).astype(BF16)
@@ -175,13 +184,13 @@
         each_pair(c, act)
 
     def finish(c):
-        def act(o, cols, qkvg):
+        def act(u, o, qkvg):
             q, k, v, g = qkvg
             for j in range(2):
-                here = pl.ds(pl.multiple_of(c * wide + o * pair + j * HD, HD), HD)
+                here = pl.ds(pl.multiple_of(u * wide + o * pair + j * HD, HD), HD)
                 at = pl.ds((o * 2 + j) * slots, slots)
-                kv = xp[c, at, 0].reshape(HD, HD)
-                rq = xp[c, at, 1].reshape(HD, HD)
+                kv = xp[u, at, 0].reshape(HD, HD)
+                rq = xp[u, at, 1].reshape(HD, HD)
                 terms = (
                     contract(part(q, j), kv, 1, 0),
                     contract(part(g, j), kv, 1, 1),
@@ -194,50 +203,54 @@
         each_pair(c, act)
 
     def stage_a(c):
-        xr[c, 0] = mine[c, head]
+        run = runs[c]
+        xr[run, 0] = mine[run, head]
         x_all(c).wait_recv()
-        total = xr[c, 0].astype(F32)
+        total = xr[run, 0].astype(F32)
         for d in range(1, NH):
-            total += xr[c, d].astype(F32)
-        cs[c] = total
+            total += xr[run, d].astype(F32)
+        cs[run] = total
         c_swap(c).start()
 
     def stage_c(c):
+        run = runs[c]
         c_swap(c).wait_recv()
-        zs[c] = cs[c, core] + cr[c]
+        zs[run] = cs[run, core] + cr[run]
         for i in range(NZ):
             @pl.when(sends_to(i))
             def _():
                 z_out(c, i).start()
 
     def stage_d(c):
-        ds[c] = jnp.zeros_like(ds[c])
+        run = runs[c]
+        ds[run] = jnp.zeros_like(ds[run])
         for i in range(NZ):
             @pl.when(hears_from(i))
             def _():
                 z_in(c, i).wait_recv()
-                ds[c] += zr[c, i]
-        zr[c, z] = ds[c]
-        ds[c] += cs[c, core]
+                ds[run] += zr[run, i]
+        zr[run, z] = ds[run]
+        ds[run] += cs[run, core]
         d_swap(c).start()
 
     def stage_e(c):
+        run = runs[c]
         d_swap(c).wait_recv()
         for kind in range(2):
-            base = jnp.where(core == kind, zr[c, z], dr[c])
+            base = jnp.where(core == kind, zr[run, z], dr[run])
             order = range(NH) if kind == 0 else range(NH - 1, -1, -1)
             for i in order:
-                xb[c, i, kind] = base.astype(BF16)
-                base = base + xr[c, slot(i), kind].astype(F32)
+                xb[run, i, kind] = base.astype(BF16)
+                base = base + xr[run, slot(i), kind].astype(F32)
         for d in ORDER:
             xb_out(c, d).start()
-        xp[c, head] = xb[c, head]
+        xp[run, head] = xb[run, head]
 
     def stage_g(c):
         xb_all(c).wait_recv()
         finish(c)
 
-    for c in range(chunks):
+    for c in chunks:
         for i in range(4):
             load(c, i).wait()
         local_states(c)
@@ -272,7 +285,7 @@
             meet_z()
         stages[name](c)
 
-    for c in range(chunks):
+    for c in chunks:
         x_all(c).wait_send()
         c_swap(c).wait_send()
         for i in range(NZ):
@@ -315,12 +328,12 @@
             vmem((CH, 2) + piece, F32), vmem((CH,) + piece, F32),
             vmem((CH,) + piece, F32), vmem((CH, NZ) + piece, F32),
             vmem((CH,) + piece, F32), vmem((CH,) + piece, F32),
-            dma((CH, 4)), pltpu.SemaphoreType.REGULAR,
-            dma((CH,)), dma((CH,)),
-            dma((CH,)), dma((CH,)),
-            dma((CH, NZ)), dma((CH, NZ)),
-            dma((CH,)), dma((CH,)),
-            dma((CH,)), dma((CH,)),
+            dma((len(CHUNKS), 4)), pltpu.SemaphoreType.REGULAR,
+            dma((len(CHUNKS),)), dma((len(CHUNKS),)),
+            dma((len(CHUNKS),)), dma((len(CHUNKS),)),
+            dma((len(CHUNKS), NZ)), dma((len(CHUNKS), NZ)),
+            dma((len(CHUNKS),)), dma((len(CHUNKS),)),
+            dma((len(CHUNKS),)), dma((len(CHUNKS),)),
         ],
         compiler_params=pltpu.CompilerParams(
             collective_id=0, has_side_effects=True, vmem_limit_bytes=54 * 2**20

time: 60.1 us -> 59.8 us (level)
  no operation moved by 1% of the time
where the time goes in v5:
time: 59.8 us; the launch traced here: 59.7 us
  Pallas kernels  59 us (99%)
  between operations  0.64 us (1%)
    pallas_call x1, Pallas kernels, on_device(): pl.pallas_call(functools.partial(kernel, scale), out_shape=[pltpu.VMEM((t...  56.3 us
    pallas_call x1, Pallas kernels, on_device(): pl.pallas_call(write_out, out_shape=[jax.ShapeDtypeStruct((tokens, width)...  2.73 us

profile of v5, /device:TPU:1, one launch (start us, length us, event | category | flops | bytes accessed | tf_op | source)
XLA Modules:
  0.0 59.7 jit_solution(10796510441393054109)
XLA Ops:
  0.6 56.3 %shard_map.75 = (bf16[192,4096]{1,0:T(8,128)(2,1)S(1)}, bf16[192,4096]{1,0:T(8,128)(2,1)S(1)}, bf16[192,4096]{1,0:T(8,128)(2,1)S(1)}, bf16[192,4096]{1,0:T(8,128)(2,1)S(1)}) custom-call(bf16[192,4096]{1,0:T(8,128)(2,1)} %q_hbm.1, bf16[192,4096]{1,0:T(8,128)(2,1)} %k_hbm.1, bf16[192,4096]{1,0:T(8,128)(2,1)} %v_hbm.1, bf16[192,4096]{1,0:T(8,128)(2,1)} %g_hbm.1), custom_call_target="tpu_custom_call" | custom-call | flops 3623878656 | bytes 12582912 | tf_op jit(solution)/shard_map/pallas_call | solution.py:320
  57.0 2.7 %shard_map.76 = (bf16[192,4096]{1,0:T(8,128)(2,1)}, bf16[192,4096]{1,0:T(8,128)(2,1)}, bf16[192,4096]{1,0:T(8,128)(2,1)}, bf16[192,4096]{1,0:T(8,128)(2,1)}) custom-call(bf16[192,4096]{1,0:T(8,128)(2,1)S(1)} %get-tuple-element.8.a, bf16[192,4096]{1,0:T(8,128)(2,1)S(1)} %get-tuple-element.9.dq, bf16[192,4096]{1,0:T(8,128)(2,1)S(1)} %get-tuple-element.10.dk, ...), custom_call_target="tpu_custom_call" | custom-call | tf_op jit(solution)/shard_map/pallas_call | solution.py:345
